TPU v7x, 32 devices: a whole 2x2x4 slice. The times are simulated.
32 devices in a mesh: head: 2 (over core), blk: 2 (over x), dp: 8 (over z, y).
Axes of the slice: x: 2, y: 2, z: 4, core: 2. Of those that a mesh axis runs over, the one named last changes fastest.
Arguments:
- layer_in: bfloat16 [32, 1024, 768], P('dp', 'blk', 'head'), may hold values from -6 to 6
- segments: int32 [32, 1024], P('dp'), may hold values from 0 to 6, as said below
- block_perm: int32 [12, 2], P('head'), may hold values from 0 to 1, as said below
- w_query: bfloat16 [768, 768], P(None, 'head'), may hold values from -0.21875 to 0.21875
- b_query: float32 [768], P('head'), may hold values from -3 to 3
- w_key: bfloat16 [768, 768], P(None, 'head'), may hold values from -0.21875 to 0.21875
- w_value: bfloat16 [768, 768], P(None, 'head'), may hold values from -0.21875 to 0.21875
- b_value: float32 [768], P('head'), may hold values from -3 to 3
- w_attn_out: bfloat16 [768, 768], P('head'), may hold values from -0.625 to 0.625
- b_attn_out: float32 [768], P('head'), may hold values from -3 to 3
- norm1_gain: float32 [768], P('head'), may hold values from 0.5 to 1.5
- norm1_bias: float32 [768], P('head'), may hold values from -3 to 3
- w_up: bfloat16 [768, 3072], P(None, 'head'), may hold values from -0.21875 to 0.21875
- b_up: float32 [3072], P('head'), may hold values from -3 to 3
- w_down: bfloat16 [3072, 768], P('head'), may hold values from -0.109375 to 0.109375
- b_down: float32 [768], P('head'), may hold values from -3 to 3
- norm2_gain: float32 [768], P('head'), may hold values from 0.5 to 1.5
- norm2_bias: float32 [768], P('head'), may hold values from -3 to 3
- grad_out: float32 [32, 1024, 768], P('dp', 'blk', 'head'), may hold values from -6 to 6
Outputs:
- layer_out: float32 [32, 1024, 768], P('dp', 'blk', 'head')
- grad_in: float32 [32, 1024, 768], P('dp', 'blk', 'head')
- grad_w_query: float32 [768, 768], P(None, 'head')
- grad_b_query: float32 [768], P('head')
- grad_w_key: float32 [768, 768], P(None, 'head')
- grad_w_value: float32 [768, 768], P(None, 'head')
- grad_b_value: float32 [768], P('head')
- grad_w_attn_out: float32 [768, 768], P('head')
- grad_b_attn_out: float32 [768], P('head')
- grad_norm1_gain: float32 [768], P('head')
- grad_norm1_bias: float32 [768], P('head')
- grad_w_up: float32 [768, 3072], P(None, 'head')
- grad_b_up: float32 [3072], P('head')
- grad_w_down: float32 [3072, 768], P('head')
- grad_b_down: float32 [768], P('head')
- grad_norm2_gain: float32 [768], P('head')
- grad_norm2_bias: float32 [768], P('head')
Inputs may be any that keep to these rules, and one draw needn't show every extreme that they name: `segments`: within each sequence the numbers start at 0 at the first position, never fall, and rise by one at six positions: three in 1 to 383 and three in 640 to 1023. `block_perm`: each row is a permutation of the block numbers; exactly 6 rows exchange the two blocks and the others keep them in place.
All inputs are finite; a program needn't handle non-finite values.
Results may differ from a plain program's by a relative error of at most 0.014.
Values may be sent and summed in bfloat16 or wider, within the bound.
A program may use at most 192 MiB of HBM per device.

v0:
```python
import functools

import jax
import jax.numpy as jnp
from jax import lax
from jax.experimental import pallas as pl
from jax.experimental.pallas import tpu as pltpu
from jax.sharding import PartitionSpec as P

EPSILON = 1e-05
NEGATIVE = -1e30
ROOT_HALF = 0.7071067811865476
DENSITY_SCALE = 0.3989422804014327
F32 = jnp.float32
BF16 = jnp.bfloat16
MIB = 1 << 20


def dot(left, right, left_dim=1, right_dim=0):
    return lax.dot_general(
        left, right, (((left_dim,), (right_dim,)), ((), ())), preferred_element_type=F32
    )


def remote(source, target, send, recv, device):
    return pltpu.make_async_remote_copy(
        src_ref=source,
        dst_ref=target,
        send_sem=send,
        recv_sem=recv,
        device_id=device,
        device_id_type=pl.DeviceIdType.MESH,
    )


def fill_bias(bias_ref, seg_ref, row, query_block, key_block):
    length = bias_ref.shape[0]

    def block(at):
        cols = pl.ds(pl.multiple_of(at * length, length), length)
        return seg_ref[pl.ds(row, 1), cols].astype(F32)

    lanes = 128
    keys = jnp.broadcast_to(block(key_block), (lanes, length)).T
    same = jnp.concatenate([keys] * (length // lanes), axis=1) == block(query_block)
    covered = jnp.max(jnp.where(same, 1.0, 0.0), axis=0, keepdims=True)
    bias_ref[...] = jnp.where(same, 0.0, covered * NEGATIVE)


def attend_pair(queries, keys, values, bias, head_width):
    pair_width = queries.shape[1]
    value_cols = values.astype(F32).T.astype(BF16)
    lane = lax.broadcasted_iota(jnp.int32, (1, pair_width), 1)
    parts, logs = [], []
    for low in range(0, pair_width, head_width):
        chosen = jnp.logical_and(lane >= low, lane < low + head_width)
        scores = dot(keys, jnp.where(chosen, queries, 0), 1, 1) + bias[...]
        top = jnp.max(scores, axis=0, keepdims=True)
        shifted = jnp.exp(scores - top)
        total = jnp.sum(shifted, axis=0, keepdims=True)
        context = dot(value_cols[low : low + head_width], shifted.astype(BF16))
        parts.append(context * (1.0 / total))
        logs.append(top + jnp.log(total))
    return jnp.concatenate(parts, axis=0).T.astype(BF16), jnp.concatenate(logs, axis=0)


def split_dot(left, right, left_dim=1, right_dim=0):
    high = left.astype(BF16)
    rest = left - high.astype(F32)
    mid = rest.astype(BF16)
    low = (rest - mid.astype(F32)).astype(BF16)
    return sum(dot(x, right, left_dim, right_dim) for x in (high, mid, low))


def front_kernel(
    head_width, scale, seqs,
    layer_hbm, gout_hbm, wq_hbm, wk_hbm, wv_hbm, wo_hbm, wup_hbm, wdn_hbm, vec_own, perm_ref,
    seg_ref,
    x_hbm, xc_hbm, q_hbm, k_hbm, v_hbm, ctx_hbm, wqs_hbm, wks_hbm, wvs_hbm, wos_hbm, sorter_hbm,
    wup_other, wdn_other, grad_hbm, vec_all, bup_all, lse_ref,
    x_ref, xc_ref, q_ref, k_ref, v_ref, ctx_ref, wn_q, wn_k, wn_v, wn_o, ws_q, ws_k, ws_v, ws_o,
    sorter_ref, sorter_t, vec_land, cross_own, cross_land, bias_ref, grad_ref, local, send, recv,
):
    head, blk = lax.axis_index("head"), lax.axis_index("blk")
    to_head, to_cross = {"head": 1 - head}, {"blk": 1 - blk}
    rows, width = x_ref.shape
    half = width // 2
    block_len = rows // seqs
    my_rows = pl.ds(pl.multiple_of(head * rows, rows), rows)
    their_rows = pl.ds(pl.multiple_of((1 - head) * rows, rows), rows)
    mine = pl.ds(pl.multiple_of(head * half, half), half)
    theirs = pl.ds(pl.multiple_of((1 - head) * half, half), half)

    started = []

    def bring(at, source, target):
        copy = pltpu.make_async_copy(source, target, local.at[at])
        copy.start()
        return copy

    def give(at, source, target, device):
        copy = remote(source, target, send.at[at], recv.at[at], device)
        copy.start()
        started.append(copy)
        return copy

    barrier = pltpu.get_barrier_semaphore()
    for device in (to_head, to_cross):
        pl.semaphore_signal(barrier, inc=1, device_id=device, device_id_type=pl.DeviceIdType.MESH)
    own_x = bring(0, layer_hbm.at[my_rows], x_ref.at[:, mine])
    own_w = [
        bring(1, wq_hbm, wn_q.at[:, :half]),
        bring(2, wk_hbm, wn_k.at[:, :half]),
        bring(3, wv_hbm, wn_v.at[:, :half]),
        bring(4, wo_hbm, wn_o.at[:half]),
    ]
    own_grad = bring(5, gout_hbm.at[my_rows], grad_ref)
    pl.semaphore_wait(barrier, 2)

    def seq_rows(seq):
        return slice(seq * block_len, (seq + 1) * block_len)

    def block_of(seq):
        return pl.ds(pl.multiple_of(head * rows + seq * block_len, block_len), block_len)

    perm = perm_ref[...]
    block = lax.broadcasted_iota(jnp.int32, perm.shape, 0)
    reads = jnp.sum(jnp.where(block == blk, perm, 0).astype(F32), axis=0, keepdims=True)
    reads = jnp.where(reads == blk.astype(F32), 0.0, 1.0)
    heads_shape = (perm.shape[1], half)
    feature_head = lax.broadcasted_iota(jnp.int32, heads_shape, 1) // head_width
    at_head = feature_head == lax.broadcasted_iota(jnp.int32, heads_shape, 0)
    cross_row = dot(
        jnp.broadcast_to(reads, (8, reads.shape[1])).astype(BF16),
        jnp.where(at_head, 1.0, 0.0).astype(BF16),
    )[0:1]
    cross_own[...] = jnp.broadcast_to(cross_row, cross_own.shape)
    flags = give(7 + 2 * seqs - 1 + 3, cross_own, cross_land, to_head)
    vecs = give(0, vec_own, vec_land, to_head)
    features = give(1, layer_hbm.at[their_rows], x_ref.at[:, mine], to_head)
    cross = [[give(2, layer_hbm.at[block_of(0)], xc_ref.at[seq_rows(0), mine], to_cross)]]
    other_w = [
        give(3, wq_hbm, wn_q.at[:, half:], to_head),
        give(4, wk_hbm, wn_k.at[:, half:], to_head),
        give(5, wv_hbm, wn_v.at[:, half:], to_head),
        give(6, wo_hbm, wn_o.at[half:], to_head),
    ]
    features.wait_recv()
    base = 7
    for seq in range(seqs):
        if seq > 0:
            cross.append(
                [give(base, layer_hbm.at[block_of(seq)], xc_ref.at[seq_rows(seq), mine], to_cross)]
            )
            base += 1
        here = seq_rows(seq)
        cross[seq].append(give(base, x_ref.at[here, theirs], xc_ref.at[here, theirs], to_cross))
        base += 1
    later = [
        give(base, wup_hbm, wup_other, to_head),
        give(base + 1, wdn_hbm, wdn_other, to_head),
        give(base + 2, gout_hbm.at[their_rows], grad_hbm.at[:, mine], to_head),
    ]

    vecs.wait_recv()
    flags.wait_recv()
    crossed = jnp.concatenate([cross_own[0:1, :], cross_land[0:1, :]], axis=1)
    row = lax.broadcasted_iota(jnp.int32, (width, width), 0)
    col = lax.broadcasted_iota(jnp.int32, (width, width), 1)
    earlier = jnp.where(row // head_width < col // head_width, 1.0, 0.0).astype(BF16)
    before = dot(jnp.broadcast_to(crossed, (8, width)).astype(BF16), earlier)[0:1]
    lane = lax.broadcasted_iota(jnp.int32, (1, width), 1)
    place = jnp.where(
        crossed > 0.5, half + before + (lane % head_width).astype(F32), lane.astype(F32) - before
    )
    found = jnp.where(row.astype(F32) == place, 1.0, 0.0)
    sorter_t[...] = found.astype(BF16)
    sorter_ref[...] = found.T.astype(BF16)
    vec_all[:, mine] = vec_own[0:8, :]
    vec_all[:, theirs] = vec_land[0:8, :]
    for at in range(bup_all.shape[1] // half):
        source = vec_own if at < 4 else vec_land
        bup_all[:, at * half : (at + 1) * half] = source[8 + at % 4 : 9 + at % 4, :]
    b_local = jnp.concatenate([vec_own[0:8, :], vec_land[0:8, :]], axis=1)
    b_sorted = split_dot(b_local, sorter_ref[...])
    bq, bv = b_sorted[6:7], b_sorted[7:8]

    own_grad.wait()
    out = [bring(17, grad_ref, grad_hbm.at[:, mine])]
    pairs_w = ((wn_q, ws_q, wqs_hbm), (wn_k, ws_k, wks_hbm), (wn_v, ws_v, wvs_hbm))
    for at, (natural, ordered, target) in enumerate(pairs_w):
        own_w[at].wait()
        other_w[at].wait_recv()
        ordered[...] = dot(natural[...], sorter_ref[...]).astype(BF16)
        out.append(bring(6 + at, ordered, target))
    out.append(bring(9, sorter_ref, sorter_hbm))
    own_x.wait()
    out.append(bring(10, x_ref, x_hbm))
    x = x_ref[...]
    q_ref[...] = ((dot(x, ws_q[...]) + bq) * scale).astype(BF16)
    out.append(bring(11, q_ref, q_hbm))
    k_ref[:, :half] = dot(x, ws_k[:, :half]).astype(BF16)
    v_ref[:, :half] = (dot(x, ws_v[:, :half]) + bv[:, :half]).astype(BF16)

    pair_width = 2 * head_width
    pairs = half // pair_width

    def attention(seq, first_pair, kind):
        here = pl.ds(pl.multiple_of(seq * block_len, block_len), block_len)
        fill_bias(bias_ref, seg_ref, head * seqs + seq, blk, 1 - blk if kind else blk)

        @pl.loop(0, pairs)
        def _(at):
            pair = first_pair + at
            cols = pl.ds(pl.multiple_of(pair * pair_width, pair_width), pair_width)
            context, logs = attend_pair(
                q_ref[here, cols], k_ref[here, cols], v_ref[here, cols], bias_ref, head_width
            )
            ctx_ref[here, cols] = context
            lse_ref[seq, pair] = logs

    @pl.loop(0, seqs)
    def _(seq):
        attention(seq, 0, 0)

    own_w[3].wait()
    other_w[3].wait_recv()
    ws_o[...] = dot(sorter_t[...], wn_o[...]).astype(BF16)
    out.append(bring(12, ws_o, wos_hbm))
    for seq in range(seqs):
        here = seq_rows(seq)
        for copy in cross[seq]:
            copy.wait_recv()
        x_cross = xc_ref[here, :]
        k_ref[here, half:] = dot(x_cross, ws_k[:, half:]).astype(BF16)
        v_ref[here, half:] = (dot(x_cross, ws_v[:, half:]) + bv[:, half:]).astype(BF16)
        attention(seq, pairs, 1)
    out.append(bring(13, xc_ref, xc_hbm))
    out.append(bring(14, k_ref, k_hbm))
    out.append(bring(15, v_ref, v_hbm))
    out.append(bring(16, ctx_ref, ctx_hbm))
    for copy in later:
        copy.wait_recv()
    for copy in out:
        copy.wait()
    for copy in started:
        copy.wait_send()


def front(layer_in, grad_out, weights, vecs, perm, segments, block_len, head_width, scale):
    width = weights[0].shape[0]
    half = width // 2
    seqs = segments.shape[0] // 2
    rows = seqs * block_len
    part = weights[4].shape[1]
    anywhere = pl.BlockSpec(memory_space=pl.ANY)
    vmem = pl.BlockSpec(memory_space=pltpu.VMEM)
    tokens = jax.ShapeDtypeStruct((rows, width), BF16)
    square = jax.ShapeDtypeStruct((width, width), BF16)
    low_rows, low_square = pltpu.VMEM((rows, width), BF16), pltpu.VMEM((width, width), BF16)
    copies = 7 + 2 * seqs - 1 + 3 + 1
    return pl.pallas_call(
        functools.partial(front_kernel, head_width, scale, seqs),
        in_specs=[anywhere] * 8 + [vmem] * 3,
        out_specs=[anywhere] * 14 + [vmem] * 3,
        out_shape=[tokens] * 6
        + [square] * 5
        + [
            jax.ShapeDtypeStruct(weights[4].shape, BF16),
            jax.ShapeDtypeStruct(weights[5].shape, BF16),
            jax.ShapeDtypeStruct((rows, width), F32),
            jax.ShapeDtypeStruct((8, width), F32),
            jax.ShapeDtypeStruct((1, 2 * part), F32),
            jax.ShapeDtypeStruct((seqs, width // (2 * head_width), 2, block_len), F32),
        ],
        scratch_shapes=[low_rows] * 6
        + [low_square] * 10
        + [
            pltpu.VMEM((16, half), F32),
            pltpu.VMEM((8, half), F32),
            pltpu.VMEM((8, half), F32),
            pltpu.VMEM((block_len, block_len), F32),
            pltpu.VMEM((rows, half), F32),
            pltpu.SemaphoreType.DMA((18,)),
            pltpu.SemaphoreType.DMA((copies,)),
            pltpu.SemaphoreType.DMA((copies,)),
        ],
        compiler_params=pltpu.CompilerParams(
            collective_id=3, has_side_effects=True, vmem_limit_bytes=60 * MIB
        ),
        name="front",
    )(layer_in, grad_out, *weights, vecs, perm, segments)


def unit_rows(rows, width):
    mean = jnp.sum(rows, axis=1, keepdims=True) * (1.0 / width)
    centered = rows - mean
    variance = jnp.sum(centered * centered, axis=1, keepdims=True) * (1.0 / width)
    inverse = lax.rsqrt(variance + EPSILON)
    return centered * inverse, inverse


def unit_back(grad, unit, inverse, gain, width):
    scaled = grad * gain
    plain = jnp.sum(scaled, axis=1, keepdims=True) * (1.0 / width)
    along = jnp.sum(scaled * unit, axis=1, keepdims=True) * (1.0 / width)
    return (scaled - plain - unit * along) * inverse


def middle_kernel(
    chunk, tiles, ctx_ref, x_ref, gout_ref, vec_ref, bup_ref, wo_hbm,
    wup0_hbm, wup1_hbm, wdn0_hbm, wdn1_hbm,
    out_ref, gattn_ref, gattnb_ref, gctx_ref, gvec_ref, gbup_ref, gwup_ref, gwdn_ref,
    slope_ref, act_ref, gup_ref, normed_t, gffn_t, wo_ref, wup0_ref, wup1_ref, wdn0_ref, wdn1_ref,
    staged, landed, local, send, recv,
):
    tile, width = x_ref.shape
    part = wup0_ref.shape[1]
    at_step = pl.program_id(0)
    to_head = {"head": 1 - lax.axis_index("head")}
    loads = [
        pltpu.make_async_copy(source, target, local.at[at])
        for at, (source, target) in enumerate(
            (
                (wo_hbm, wo_ref), (wup0_hbm, wup0_ref), (wdn0_hbm, wdn0_ref),
                (wup1_hbm, wup1_ref), (wdn1_hbm, wdn1_ref),
            )
        )
    ]

    @pl.when(at_step == 0)
    def _():
        for load in loads:
            load.start()
        barrier = pltpu.get_barrier_semaphore()
        pl.semaphore_signal(
            barrier, inc=1, device_id=to_head, device_id_type=pl.DeviceIdType.MESH
        )
        for load in loads:
            load.wait()
        pl.semaphore_wait(barrier, 1)
        gvec_ref[...] = jnp.zeros_like(gvec_ref)
        gbup_ref[...] = jnp.zeros_like(gbup_ref)

    def vec(i):
        return vec_ref[i : i + 1, :]

    def add_vec(i, rows):
        gvec_ref[i : i + 1, :] += jnp.sum(rows, axis=0, keepdims=True)

    @pl.when(at_step < tiles)
    def _():
        here = pl.ds(pl.multiple_of(at_step * tile, tile), tile)
        attended = dot(ctx_ref[...], wo_ref[...])
        unit1, inverse1 = unit_rows(x_ref[...].astype(F32) + attended + vec(0), width)
        normed = unit1 * vec(1) + vec(2)
        normed_low = normed.astype(BF16)
        normed_t[:, here] = normed_low.T
        pieces = ((wup0_ref, wdn0_ref), (wup1_ref, wdn1_ref))
        down = jnp.zeros_like(normed)
        for at, (wup, wdn) in enumerate(pieces):
            for low in range(0, part, chunk):
                cols = slice(at * part + low, at * part + low + chunk)
                up = dot(normed_low, wup[:, low : low + chunk]) + bup_ref[:, cols]
                cumulative = 0.5 + 0.5 * lax.erf(up * ROOT_HALF)
                slope_ref[:, cols] = cumulative + up * (jnp.exp(-0.5 * up * up) * DENSITY_SCALE)
                activated = (up * cumulative).astype(BF16)
                act_ref[here, cols] = activated
                down += dot(activated, wdn[low : low + chunk, :])
        unit2, inverse2 = unit_rows(normed + down + vec(3), width)
        out_ref[...] = unit2 * vec(4) + vec(5)
        grad_out = gout_ref[...]
        add_vec(4, grad_out * unit2)
        add_vec(5, grad_out)
        grad_ffn = unit_back(grad_out, unit2, inverse2, vec(4), width)
        add_vec(3, grad_ffn)
        grad_ffn_low = grad_ffn.astype(BF16)
        gffn_t[:, here] = grad_ffn_low.T
        back = jnp.zeros_like(normed)
        for at, (wup, wdn) in enumerate(pieces):
            for low in range(0, part, chunk):
                cols = slice(at * part + low, at * part + low + chunk)
                grad_act = dot(grad_ffn_low, wdn[low : low + chunk, :], 1, 1)
                grad_up = (grad_act * slope_ref[:, cols]).astype(BF16)
                gup_ref[here, cols] = grad_up
                gbup_ref[0:1, cols] += jnp.sum(grad_up.astype(F32), axis=0, keepdims=True)
                back += dot(grad_up, wup[:, low : low + chunk], 1, 1)
        grad_mid = grad_ffn + back
        add_vec(1, grad_mid * unit1)
        add_vec(2, grad_mid)
        grad_attn = unit_back(grad_mid, unit1, inverse1, vec(1), width)
        add_vec(0, grad_attn)
        gattn_ref[...] = grad_attn
        grad_attn_low = grad_attn.astype(BF16)
        gattnb_ref[...] = grad_attn_low
        gctx_ref[...] = dot(grad_attn_low, wo_ref[...], 1, 1).astype(BF16)

    cols_step = gwup_ref.shape[1]
    count = part // cols_step

    def gradients(low):
        cols = pl.ds(pl.multiple_of(low, cols_step), cols_step)
        return dot(normed_t[...], gup_ref[:, cols]), dot(gffn_t[...], act_ref[:, cols])

    def exchange(slot):
        return remote(staged.at[slot], landed.at[slot], send.at[slot], recv.at[slot], to_head)

    @pl.when(jnp.logical_and(at_step >= tiles, at_step < tiles + count))
    def _():
        at = at_step - tiles
        for kind, value in enumerate(gradients(part + at * cols_step)):
            staged[kind * count + at] = value.astype(BF16)
            exchange(kind * count + at).start()

    @pl.when(at_step >= tiles + count)
    def _():
        at = at_step - tiles - count
        found = gradients(at * cols_step)
        for kind, (value, target) in enumerate(zip(found, (gwup_ref, gwdn_ref))):
            exchange(kind * count + at).wait()
            target[...] = (value + landed[kind * count + at].astype(F32)).astype(BF16)


def middle(ctx, x, grad_out, vectors, b_up, w_out, w_up, w_down):
    rows, width = x.shape
    part = w_up[0].shape[1]
    tile = 256
    tiles = rows // tile
    chunk = part // 2
    cols_step = part // 3

    def tiled(cols):
        return pl.BlockSpec((tile, cols), lambda i: (jnp.minimum(i, tiles - 1), 0))

    def whole(array):
        return pl.BlockSpec(array.shape, lambda i: (0, 0), pipeline_mode=pl.Buffered(1))

    def shape(cols, kind):
        return jax.ShapeDtypeStruct((rows, cols), kind)

    outs = [(width, F32), (width, F32), (width, BF16), (width, BF16)]
    sums = [jax.ShapeDtypeStruct((8, width), F32), jax.ShapeDtypeStruct((8, b_up.shape[1]), F32)]
    grads = [jax.ShapeDtypeStruct((width, part), BF16)] * 2
    count = part // cols_step
    grad_spec = pl.BlockSpec((width, cols_step), lambda i: (0, jnp.maximum(i - tiles - count, 0)))
    slots = pltpu.VMEM((2 * count, width, cols_step), BF16)
    weights = [vectors, b_up, w_out, *w_up, *w_down]
    return pl.pallas_call(
        functools.partial(middle_kernel, chunk, tiles),
        grid=(tiles + 2 * part // cols_step,),
        in_specs=[tiled(width), tiled(width), tiled(width)]
        + [whole(vectors), whole(b_up)]
        + [pl.BlockSpec(memory_space=pl.ANY)] * 5,
        out_specs=[tiled(c) for c, _ in outs]
        + [pl.BlockSpec(s.shape, lambda i: (0, 0)) for s in sums]
        + [grad_spec] * 2,
        out_shape=[shape(c, k) for c, k in outs] + sums + grads,
        scratch_shapes=[
            pltpu.VMEM((tile, 2 * part), F32),
            pltpu.VMEM((rows, 2 * part), BF16),
            pltpu.VMEM((rows, 2 * part), BF16),
            pltpu.VMEM((width, rows), BF16),
            pltpu.VMEM((width, rows), BF16),
        ]
        + [pltpu.VMEM(w.shape, BF16) for w in weights[2:]]
        + [slots, slots]
        + [pltpu.SemaphoreType.DMA((5,))]
        + [pltpu.SemaphoreType.DMA((2 * count,))] * 2,
        compiler_params=pltpu.CompilerParams(
            collective_id=4, has_side_effects=True, vmem_limit_bytes=62 * MIB
        ),
        name="middle",
    )(ctx, x, grad_out, *weights)


LINKS = {
    "head": (("core", 1),),
    "x": (("x", 1),),
    "y": (("y", 1),),
    "u": (("outer", 1),),
    "w": (("outer", 1), ("inner", 2)),
    "group": (("group", 1),),
}
RATES = {"core": 500e3, "x": 46e3, "y": 46e3, "outer": 46e3, "inner": 46e3, "group": 46e3}
DELAY = 4.5
OP_TIME = 0.3
URGENCY = 1.0
AHEAD = 5.0
ORDERS = {
    "A": "xyuw", "B": "yxuw", "C": "uwxy", "D": "uxyw", "E": "xuyw", "F": "yuxw", "G": "uyxw",
    "H": "uwyx",
}


class Item:
    action = None
    later = 0

    def __init__(self, at, array, first, cols, rows, order, groups, from_head):
        self.at, self.array, self.first, self.cols, self.rows = at, array, first, cols, rows
        self.groups = groups
        self.sums = []
        size = rows
        for axis in [*ORDERS[order]] + (["group"] if groups > 1 else []):
            before = size
            size = size if axis == "group" else size // 2
            self.sums.append((axis, before, size))
        self.size = size
        self.stages = (
            [("head", "head", rows, rows)] * from_head
            + [("sum", *s) for s in self.sums]
            + [("result", *s) for s in reversed(self.sums) if s[0] != "group"]
        )

    def load(self, stage):
        kind, axis, before, size = self.stages[stage]
        moved = size * (self.groups - 1 if axis == "group" else 1)
        return axis, moved * self.cols * 2


def plan(items, steps, ready):
    free = {link: 0.0 for link in RATES}
    due = {i: (0.0, 0) for i in range(len(items))}
    batches = []
    now = 0.0

    def links(index, stage):
        item = items[index]
        return LINKS[item.load(stage)[0]] if stage < len(item.stages) else ()

    behind = []
    for index, item in enumerate(items):
        times = [
            DELAY + max(t * item.load(k)[1] / RATES[link] for link, t in links(index, k))
            for k in range(len(item.stages))
        ]
        behind.append([sum(times[k:]) for k in range(len(times) + 1)])

    def rank(i):
        return due[i][0] - URGENCY * behind[i][due[i][1]]

    def opens(i):
        return max([due[i][0]] + [free[link] - AHEAD for link, _ in links(i, due[i][1])])

    def run(index, batch):
        nonlocal now
        stage = due[index][1]
        batch.append((index, stage))
        now += OP_TIME
        if stage == len(items[index].stages):
            del due[index]
            return
        size = items[index].load(stage)[1]
        end = now
        for link, times in links(index, stage):
            free[link] = max(free[link], now) + times * size / RATES[link]
            end = max(end, free[link])
        due[index] = (end + DELAY, stage + 1)

    for at, time in enumerate([0.0] + steps):
        now += time
        batch = []
        while True:
            able = [
                i
                for i in due
                if opens(i) <= now and at >= (items[i].later if due[i][1] else ready[i])
            ]
            if not able:
                break
            run(min(able, key=rank), batch)
        batches.append(batch)
    while due:
        here = [i for i in due if opens(i) <= now]
        first = min(here, key=rank) if here else min(due, key=lambda i: (opens(i), i))
        now = max(now, opens(first))
        run(first, batches[-1])
    return batches


class Places:
    def __init__(self, groups):
        head, blk, dp = lax.axis_index("head"), lax.axis_index("blk"), lax.axis_index("dp")
        group = dp // 8
        self.head = head
        self.bit = {"x": blk, "y": dp % 2, "u": (dp // 2) % 2, "w": (dp // 4) % 2}
        self.partners = {
            "head": [{"head": 1 - head}],
            "x": [{"blk": 1 - blk}],
            "y": [{"dp": dp + 1 - 2 * self.bit["y"]}],
            "u": [{"dp": dp + 2 - 4 * self.bit["u"]}],
            "w": [{"dp": dp + 4 - 8 * self.bit["w"]}],
            "group": [{"dp": (group + d) % groups * 8 + dp % 8} for d in range(1, groups)],
        }

    def greet(self):
        barrier = pltpu.get_barrier_semaphore()
        everyone = [device for devices in self.partners.values() for device in devices]
        for device in everyone:
            pl.semaphore_signal(
                barrier, inc=1, device_id=device, device_id_type=pl.DeviceIdType.MESH
            )
        pl.semaphore_wait(barrier, len(everyone))


SUM_SLOT = {"x": 1, "y": 2, "u": 3, "w": 4, "group": 9}
RESULT_SLOT = {"x": 5, "y": 6, "u": 7, "w": 8}


def slot_count(groups):
    return 9 + groups - 1


class Sums:
    def __init__(
        self, items, places, own, other, total, result, final, landing, send, recv, store
    ):
        self.items, self.places, self.final, self.store = items, places, final, store
        self.own, self.other, self.total, self.result = own, other, total, result
        self.landing, self.send, self.recv = landing, send, recv
        self.sent = []

    def start_of(self, item, stop):
        start = 0
        for name, before, after in item.sums:
            if name == stop:
                return start
            start = self.within(start, name, after)
        return start

    def within(self, start, axis, after):
        if axis == "group":
            return start
        return start + self.places.bit[axis] * after

    def part(self, ref, start, size, item):
        return ref.at[
            pl.ds(pl.multiple_of(start, 16), size), item.first : item.first + item.cols
        ]

    def copies_of(self, item, stage):
        kind, axis, before, after = item.stages[stage]
        devices = self.places.partners[axis]
        out = []

        def add(source, target, slot, device):
            out.append(
                remote(
                    source, target, self.send.at[item.at, slot], self.recv.at[item.at, slot], device
                )
            )

        if kind == "head":
            cols = slice(item.first, item.first + item.cols)
            add(self.other[item.array].at[:, cols], self.total[item.array].at[:, cols], 0, devices[0])
            return out
        if kind == "sum":
            start = self.start_of(item, axis)
            ref = self.total[item.array]
            buf = self.landing[item.at][axis]
            for d, device in enumerate(devices):
                if axis == "group":
                    row = start
                else:
                    row = start + (1 - self.places.bit[axis]) * after
                add(self.part(ref, row, after, item), buf.at[d], SUM_SLOT[axis] + d, device)
            return out
        start, size = self.held(item, stage)
        here = self.part(self.result[item.array], start, size, item)
        for device in devices:
            add(here, here, RESULT_SLOT[axis], device)
        return out

    def held(self, item, stage):
        start, size = self.start_of(item, None), item.size
        for kind, axis, before, after in item.stages[:stage]:
            if kind == "result":
                start, size = self.start_of(item, axis), before
        return start, size

    def op(self, index, stage):
        item = self.items[index]
        if item.action is not None:
            item.action(stage)
            if stage < len(item.stages):
                self.sent.append((item, stage))
            return
        if stage > 0:
            kind, axis, before, after = item.stages[stage - 1]
            copies = self.copies_of(item, stage - 1)
            for copy in copies:
                copy.wait_recv()
            if kind == "head":
                cols = slice(item.first, item.first + item.cols)
                total = self.total[item.array]
                total[:, cols] = (
                    self.own[item.array][:, cols].astype(F32) + total[:, cols].astype(F32)
                ).astype(BF16)
            elif kind == "sum":
                start = self.within(self.start_of(item, axis), axis, after)
                here = self.part(self.total[item.array], start, after, item)
                value = here[...].astype(F32)
                for d in range(len(copies)):
                    value = value + self.landing[item.at][axis][d].astype(F32)
                if item.stages[stage][0] != "result":
                    here[...] = value.astype(BF16)
                else:
                    self.part(self.result[item.array], start, after, item)[...] = value.astype(BF16)
        if stage < len(item.stages):
            for copy in self.copies_of(item, stage):
                copy.start()
            self.sent.append((item, stage))
        else:
            self.store_of(item).start()

    def store_of(self, item):
        cols = slice(item.first, item.first + item.cols)
        return pltpu.make_async_copy(
            self.result[item.array].at[:, cols], self.final[item.array].at[:, cols],
            self.store.at[item.at],
        )

    def finish(self):
        for item in self.items:
            if item.action is None and self.sent:
                self.store_of(item).wait()
        for item, stage in self.sent:
            copies = self.copies_of(item, stage) if item.action is None else item.copies(stage)
            for copy in copies:
                copy.wait_send()


class Other:
    def __init__(self, loads):
        self.stages, self.action, self.copies = loads, None, None
        self.later = 0

    def load(self, stage):
        return self.stages[stage]


def landing_shapes(items):
    shapes = []
    for item in items:
        if isinstance(item, Other):
            continue
        for kind, axis, before, after in item.stages:
            if kind == "sum":
                slots = item.groups - 1 if axis == "group" else 1
                shapes.append((item.at, axis, (slots, after, item.cols)))
    return shapes


def make_items(arrays, rows, cols, orders, groups, from_head, at=0):
    items = []
    step = len(arrays) * cols // len(orders)
    for index in range(len(orders)):
        array, first = divmod(index * step, cols)
        items.append(
            Item(at + index, arrays[array], first, step, rows, orders[index], groups, from_head)
        )
    return items


def run_batch(sums, batch):
    for index, stage in batch:
        sums.op(index, stage)


FFN_ORDERS = "GGAAAFFB"
HEAD_ORDERS = "DBDBBA"
MOVES = 4


def small_axes(groups):
    return ("x", "y", "u", "w") + (("group",) if groups > 1 else ())


def small_slot(axis):
    return 3 + {"x": 0, "y": 1, "u": 2, "w": 3, "group": 4}[axis]


def back_kernel(
    items, batches, groups, head_width, scale,
    up_hbm, down_hbm, q_hbm, k_hbm, v_hbm, g_hbm, x_hbm, xc_hbm, ctx_hbm, gattnb_hbm, gattn_hbm,
    wq_hbm, wk_hbm, wv_hbm, sorter_hbm, rows_hbm, lse_ref, seg_ref, gvec_ref, gbup_ref,
    out_up, out_down, out_heads, small_ref, din_all, rows_all,
    res_up, res_down, res_heads, total_up, total_down, total_heads, heads_own, heads_other,
    q_ref, k_ref, v_ref, g_ref, x_ref, xc_ref, ctx_ref, gattnb_ref, dx_ref, wq_ref, wk_ref, wv_ref,
    sorter_ref, bias_ref, gwo_ref, bsum_ref, dxc_ref, cross_land, small_land, small_stage,
    send, recv, small_send, small_recv, move_send, move_recv, local, store, *landing_refs,
):
    places = Places(groups)
    tokens, width = x_ref.shape
    block_len = bias_ref.shape[0]
    seqs = tokens // block_len
    blk = places.bit["x"]
    half = width // 2
    part = gbup_ref.shape[1] // 2
    head = places.head
    mine_cols = pl.ds(pl.multiple_of(head * half, half), half)
    their_cols = pl.ds(pl.multiple_of((1 - head) * half, half), half)

    pairs_in = [
        (up_hbm, total_up), (down_hbm, total_down),
        (q_hbm, q_ref), (k_hbm, k_ref), (v_hbm, v_ref), (g_hbm, g_ref),
        (wk_hbm, wk_ref), (wv_hbm, wv_ref), (x_hbm, x_ref), (xc_hbm, xc_ref), (ctx_hbm, ctx_ref),
        (gattnb_hbm, gattnb_ref), (sorter_hbm, sorter_ref), (gattn_hbm, dx_ref), (wq_hbm, wq_ref),
    ]
    loads = [
        pltpu.make_async_copy(source, target, local.at[at])
        for at, (source, target) in enumerate(pairs_in)
    ]
    for load in loads:
        load.start()
    places.greet()
    landing = {}
    for (at, axis, _), ref in zip(landing_shapes(items), landing_refs):
        landing.setdefault(at, {})[axis] = ref
    sums = Sums(
        items, places, {2: heads_own}, {2: heads_other}, [total_up, total_down, total_heads],
        [res_up, res_down, res_heads], [out_up, out_down, out_heads], landing, send, recv, store,
    )

    each = tokens // MOVES

    def kept(at):
        return pl.ds(pl.multiple_of(head * tokens + at * each, each), each)

    my_rows = pl.ds(pl.multiple_of(head * tokens, tokens), tokens)

    def rows_copy():
        return remote(
            rows_hbm.at[:, their_cols], rows_all.at[my_rows], move_send.at[2 * MOVES],
            move_recv.at[2 * MOVES], places.partners["head"][0],
        )

    rows_keep = pltpu.make_async_copy(
        rows_hbm.at[:, mine_cols], rows_all.at[my_rows], local.at[len(pairs_in) + MOVES]
    )
    rows_keep.start()

    def cross_copy(at):
        here = slice(at * each, (at + 1) * each)
        return remote(
            dxc_ref.at[here], cross_land.at[here], move_send.at[at], move_recv.at[at],
            places.partners["x"][0],
        )

    def head_copy(at):
        here = slice(at * each, (at + 1) * each)
        return remote(
            dx_ref.at[here, their_cols], din_all.at[kept(at)], move_send.at[MOVES + at],
            move_recv.at[MOVES + at], places.partners["head"][0],
        )

    def keep_copy(at):
        here = slice(at * each, (at + 1) * each)
        return pltpu.make_async_copy(
            dx_ref.at[here, mine_cols], din_all.at[kept(at)], local.at[len(pairs_in) + at]
        )

    def move_copies(at, stage):
        return [cross_copy(at) if stage == 0 else head_copy(at)]

    def move(at, stage):
        here = slice(at * each, (at + 1) * each)
        if stage == 0:
            cross_copy(at).start()
        elif stage == 1:
            cross_copy(at).wait_recv()
            dx_ref[here, :] = dx_ref[here, :] + cross_land[here, :].astype(F32)
            head_copy(at).start()
            keep_copy(at).start()
        else:
            head_copy(at).wait_recv()
            keep_copy(at).wait()

    axes = small_axes(groups)

    def small_copies(stage):
        if stage == 0:
            device = places.partners["head"][0]
            spans = (
                (gvec_ref.at[:, their_cols], slice(0, half)),
                (bsum_ref.at[:, half:], slice(half, 2 * half)),
                (gbup_ref.at[:, part:], slice(2 * half, 2 * half + part)),
            )
            return [
                remote(
                    source, small_land.at[at, :, span], small_send.at[at], small_recv.at[at], device
                )
                for at, (source, span) in enumerate(spans)
            ]
        first = small_slot(axes[stage - 1])
        return [
            remote(
                small_stage.at[stage], small_land.at[first + d], small_send.at[first + d],
                small_recv.at[first + d], device,
            )
            for d, device in enumerate(places.partners[axes[stage - 1]])
        ]

    def small(stage):
        if stage == 1:
            for copy in small_copies(0):
                copy.wait_recv()
            small_stage[1, :, :half] = gvec_ref[:, mine_cols] + small_land[0, :, :half]
            small_stage[1, :, half : 2 * half] = (
                bsum_ref[:, :half] + small_land[1, :, half : 2 * half]
            )
            small_stage[1, :, 2 * half :] = gbup_ref[:, :part] + small_land[2, :, 2 * half :]
        elif stage > 1:
            value = small_stage[stage - 1]
            first = small_slot(axes[stage - 2])
            for d, copy in enumerate(small_copies(stage - 1)):
                copy.wait_recv()
                value = value + small_land[first + d]
            if stage <= len(axes):
                small_stage[stage] = value
            else:
                small_ref[...] = value
        if stage <= len(axes):
            for copy in small_copies(stage):
                copy.start()

    others = [item for item in items if isinstance(item, Other)]
    others[0].action, others[0].copies = small, small_copies
    for at, item in enumerate(others[1:]):
        item.action = functools.partial(move, at)
        item.copies = functools.partial(move_copies, at)

    pair_width = 2 * head_width
    pairs = width // pair_width
    batches = list(batches)
    for at in (0, 1):
        loads[at].wait()
    run_batch(sums, batches.pop(0))

    def steps(count, body):
        last = len(batches) == count

        @pl.loop(0, count)
        def _(step):
            body(step)
            for at in range(count - 1 if last else count):
                if batches[at]:
                    @pl.when(step == at)
                    def _():
                        run_batch(sums, batches[at])

        if last:
            run_batch(sums, batches[-1])
        del batches[:count]

    def attention(crossed, step):
        seq = step // (pairs // 2)
        pair = crossed * (pairs // 2) + step % (pairs // 2)
        here = pl.ds(pl.multiple_of(seq * block_len, block_len), block_len)
        cols = pl.ds(pl.multiple_of(pair * pair_width, pair_width), pair_width)

        @pl.when(step % (pairs // 2) == 0)
        def _():
            fill_bias(bias_ref, seg_ref, head * seqs + seq, blk, 1 - blk if crossed else blk)

        queries, keys = q_ref[here, cols], k_ref[here, cols]
        values, grads = v_ref[here, cols], g_ref[here, cols]
        logs = lse_ref[seq, pair]
        key_cols = keys.astype(F32).T.astype(BF16)
        lane = lax.broadcasted_iota(jnp.int32, (1, pair_width), 1)
        query_parts = []
        for at, low in enumerate(range(0, pair_width, head_width)):
            chosen = jnp.logical_and(lane >= low, lane < low + head_width)
            scores = dot(keys, jnp.where(chosen, queries, 0), 1, 1) + bias_ref[...]
            mixing = jnp.exp(scores - logs[at : at + 1, :])
            grad_mixing = dot(values, jnp.where(chosen, grads, 0), 1, 1)
            inner = jnp.sum(mixing * grad_mixing, axis=0, keepdims=True)
            grad_scores = (mixing * (grad_mixing - inner)).astype(BF16)
            grad_value = dot(mixing.astype(BF16), grads)
            grad_key = dot(grad_scores, queries)
            query_parts.append(dot(key_cols[low : low + head_width], grad_scores))
            if at == 0:
                all_value, all_key = grad_value, grad_key
            else:
                all_value = jnp.where(chosen, grad_value, all_value)
                all_key = jnp.where(chosen, grad_key, all_key)
        q_ref[here, cols] = (jnp.concatenate(query_parts, axis=0).T.astype(BF16) * scale).astype(
            BF16
        )
        k_ref[here, cols] = all_key.astype(BF16)
        v_ref[here, cols] = all_value.astype(BF16)

    tile = 256

    def tile_of(step):
        return pl.ds(pl.multiple_of(step * tile, tile), tile)

    def cross_inputs(step):
        here = tile_of(step)
        dxc_ref[here, :] = (
            dot(k_ref[here, half:], wk_ref[:, half:], 1, 1)
            + dot(v_ref[here, half:], wv_ref[:, half:], 1, 1)
        ).astype(BF16)

    for at in range(2, 6):
        loads[at].wait()
    steps(seqs * pairs // 2, functools.partial(attention, 1))
    for at in (6, 7):
        loads[at].wait()
    steps(tokens // tile, cross_inputs)
    steps(seqs * pairs // 2, functools.partial(attention, 0))
    for at in range(8, 13):
        loads[at].wait()

    def weights(step):
        mine = tile_of(step)
        left, left_cross = x_ref[:, mine].T, xc_ref[:, mine].T
        for at, ref in enumerate((q_ref, k_ref, v_ref)):
            first = dot(left, ref[:, :half])
            second = dot(left if at == 0 else left_cross, ref[:, half:])
            found = jnp.concatenate([first, second], axis=1).astype(BF16)
            natural = dot(found, sorter_ref[...], 1, 1).astype(BF16)
            heads_own[mine, at * half : (at + 1) * half] = natural[:, :half]
            heads_other[mine, at * half : (at + 1) * half] = natural[:, half:]
        gwo_ref[mine, :] = dot(ctx_ref[:, mine].T, gattnb_ref[...]).astype(BF16)

    steps(width // tile, weights)

    def last_weight(_):
        for ref, low in ((heads_own, 0), (heads_other, half)):
            natural = dot(sorter_ref[low : low + half], gwo_ref[...]).astype(BF16)
            ref[:half, 3 * half :] = natural[:, :half]
            ref[half:, 3 * half :] = natural[:, half:]
        totals = []
        for ref in (q_ref, v_ref):
            totals.append(jnp.sum(ref[...].astype(F32), axis=0, keepdims=True))
        found = jnp.concatenate(totals + [jnp.zeros((6, width), F32)], axis=0)
        high = found.astype(BF16)
        rest = found - high.astype(F32)
        middle_part = rest.astype(BF16)
        rest = rest - middle_part.astype(F32)
        bsum_ref[...] = (
            dot(high, sorter_ref[...], 1, 1)
            + dot(middle_part, sorter_ref[...], 1, 1)
            + dot(rest.astype(BF16), sorter_ref[...], 1, 1)
        )

    steps(1, last_weight)
    rows_copy().start()
    for at in range(13, 15):
        loads[at].wait()

    def inputs(step):
        here = tile_of(step)
        dq, dk, dv = q_ref[here, :], k_ref[here, :], v_ref[here, :]
        dx_ref[here, :] = (
            dx_ref[here, :]
            + dot(dq, wq_ref[...], 1, 1)
            + dot(dk[:, :half], wk_ref[:, :half], 1, 1)
            + dot(dv[:, :half], wv_ref[:, :half], 1, 1)
        )

    steps(tokens // tile, inputs)
    assert not batches
    rows_keep.wait()
    rows_copy().wait()
    sums.finish()


def attention_back(
    grads, tokens, weights, out_rows, logs, segments, grad_vecs, grad_bup, block_len, head_width,
    scale, groups,
):
    rows, cols = grads[0].shape
    count, width = tokens[0].shape
    seqs = count // block_len
    items = make_items([0, 1], rows, cols, FFN_ORDERS, groups, False)
    items += make_items([2], rows, cols, HEAD_ORDERS, groups, True, len(items))
    pair_steps = seqs * width // (2 * head_width)
    tiles, weight_steps = count // 256, width // 256
    half_steps = pair_steps // 2
    times = (
        [2.3] * half_steps + [0.9] * tiles + [2.3] * half_steps + [4.0] * weight_steps + [1.5]
        + [1.1] * tiles
    )
    heads_at = pair_steps + tiles + weight_steps + 1
    ready = [0] * len(FFN_ORDERS) + [heads_at] * len(HEAD_ORDERS)
    small = (8, width + cols)
    items.append(Other([("head", 1e4)] + [(axis, 7e4) for axis in small_axes(groups)]))
    ready.append(heads_at)
    for at in range(MOVES):
        items.append(Other([("x", count // MOVES * width * 2), ("head", count // MOVES * width * 2)]))
        items[-1].later = heads_at + (at + 1) * tiles // MOVES
        ready.append(half_steps + (at + 1) * tiles // MOVES)
    batches = plan(items, times, ready)
    landing = landing_shapes(items)
    vmem = pl.BlockSpec(memory_space=pltpu.VMEM)
    anywhere = pl.BlockSpec(memory_space=pl.ANY)
    slots = len(FFN_ORDERS) + len(HEAD_ORDERS)
    small_slots = 7 + groups - 1
    big = pltpu.VMEM((rows, cols), BF16)
    rows_low = pltpu.VMEM((count, width), BF16)
    square = pltpu.VMEM((width, width), BF16)
    large = [*grads, *tokens, *weights, out_rows]
    return pl.pallas_call(
        functools.partial(back_kernel, items, batches, groups, head_width, scale),
        in_specs=[anywhere] * len(large) + [vmem] * 4,
        out_specs=[anywhere] * 3 + [vmem] + [anywhere] * 2,
        out_shape=[jax.ShapeDtypeStruct((rows, cols), BF16)] * 3
        + [jax.ShapeDtypeStruct(small, F32)]
        + [jax.ShapeDtypeStruct((2 * count, width // 2), F32)] * 2,
        scratch_shapes=[big] * 8
        + [rows_low] * 8
        + [pltpu.VMEM((count, width), F32)]
        + [square] * 4
        + [pltpu.VMEM((block_len, block_len), F32), square, pltpu.VMEM((8, width), F32)]
        + [rows_low] * 2
        + [pltpu.VMEM((small_slots, *small), F32), pltpu.VMEM((6, *small), F32)]
        + [pltpu.SemaphoreType.DMA((slots, slot_count(groups)))] * 2
        + [pltpu.SemaphoreType.DMA((small_slots,))] * 2
        + [pltpu.SemaphoreType.DMA((2 * MOVES + 1,))] * 2
        + [pltpu.SemaphoreType.DMA((len(large) + MOVES + 1,)), pltpu.SemaphoreType.DMA((slots,))]
        + [pltpu.VMEM(shape, BF16) for _, _, shape in landing],
        compiler_params=pltpu.CompilerParams(
            collective_id=1, has_side_effects=True, vmem_limit_bytes=63 * MIB
        ),
        name="attention_back",
    )(*large, logs, segments, grad_vecs, grad_bup)


def finish_kernel(moved, up_ref, down_ref, heads_ref, *refs):
    sources, refs = refs[:moved], refs[moved:]
    gup_ref, gdown_ref, gq_ref, gk_ref, gv_ref, go_ref, *targets = refs
    width = gq_ref.shape[1]
    gup_ref[...] = up_ref[...].astype(F32)
    gdown_ref[...] = down_ref[...].astype(F32).T
    for at, ref in enumerate((gq_ref, gk_ref, gv_ref, go_ref)):
        ref[...] = heads_ref[:, at * width : (at + 1) * width].astype(F32)
    for source, target in zip(sources, targets):
        target[...] = source[...]


def finish(up, down, heads, moved):
    rows, cols = up.shape
    steps = 4
    tile = rows // steps
    half, quarter = cols // 2, cols // 4
    spec = pl.BlockSpec((tile, cols), lambda i: (i, 0))
    third = pl.BlockSpec((tile, quarter), lambda i: (i, 0))
    moves = [
        pl.BlockSpec((array.shape[0] // steps, array.shape[1]), lambda i: (i, 0)) for array in moved
    ]
    return pl.pallas_call(
        functools.partial(finish_kernel, len(moved)),
        grid=(steps,),
        in_specs=[spec, pl.BlockSpec((rows, cols // steps), lambda i: (0, i)), spec] + moves,
        out_specs=[
            spec,
            pl.BlockSpec((cols // steps, rows), lambda i: (i, 0)),
            third,
            third,
            third,
            pl.BlockSpec((tile, quarter), lambda i: (i % (steps // 2), i // (steps // 2))),
        ]
        + moves,
        out_shape=[
            jax.ShapeDtypeStruct((rows, cols), F32),
            jax.ShapeDtypeStruct((cols, rows), F32),
            jax.ShapeDtypeStruct((rows, quarter), F32),
            jax.ShapeDtypeStruct((rows, quarter), F32),
            jax.ShapeDtypeStruct((rows, quarter), F32),
            jax.ShapeDtypeStruct((rows // 2, half), F32),
        ]
        + [jax.ShapeDtypeStruct(array.shape, array.dtype) for array in moved],
        compiler_params=pltpu.CompilerParams(vmem_limit_bytes=63 * MIB),
        name="finish",
    )(up, down, heads, *moved)


def on_device(
    layer_in, segments, block_perm, w_query, b_query, w_key, w_value, b_value, w_attn_out,
    b_attn_out, norm1_gain, norm1_bias, w_up, b_up, w_down, b_down, norm2_gain, norm2_bias,
    grad_out,
):
    _, block_len, half = layer_in.shape
    head_width = w_query.shape[1] // block_perm.shape[0]
    scale = head_width ** (-0.5)

    row = lax.broadcasted_iota(jnp.int32, (16, half), 0)
    vecs = jnp.pad(b_up.reshape(-1, half), ((8, 16 - 8 - b_up.shape[0] // half), (0, 0)))
    listed = [
        b_attn_out, norm1_gain, norm1_bias, b_down, norm2_gain, norm2_bias, b_query, b_value,
    ]
    for at, vec in enumerate(listed):
        vecs = jnp.where(row == at, vec[None, :], vecs)
    (
        x, x_cross, queries, keys, values, ctx, wq, wk, wv, wo, sorter, up_other, down_other,
        grad_rows, vectors, b_up_all, logs,
    ) = front(
        layer_in.reshape(-1, half),
        grad_out.reshape(-1, half),
        (w_query, w_key, w_value, w_attn_out, w_up, w_down),
        vecs,
        block_perm.T,
        segments,
        block_len,
        head_width,
        scale,
    )
    (
        out_rows, grad_attn, grad_attn_low, grad_ctx, grad_vecs, grad_bup, grad_up_all,
        grad_down_all,
    ) = middle(
        ctx, x, grad_rows, vectors, b_up_all, wo, (w_up, up_other), (w_down, down_other)
    )
    total_up, total_down, total_heads, small, grad_in, layer_out = attention_back(
        (grad_up_all, grad_down_all),
        (queries, keys, values, grad_ctx, x, x_cross, ctx, grad_attn_low, grad_attn),
        (wq, wk, wv, sorter),
        out_rows,
        logs,
        segments,
        grad_vecs,
        grad_bup,
        block_len,
        head_width,
        scale,
        lax.axis_size("dp") // 8,
    )
    grad_up, grad_down, grad_q, grad_k, grad_v, grad_o, grad_in, layer_out = finish(
        total_up, total_down, total_heads, (grad_in, layer_out)
    )
    return (
        layer_out.reshape(layer_in.shape),
        grad_in.reshape(layer_in.shape),
        grad_q,
        small[0, half : 2 * half],
        grad_k,
        grad_v,
        small[1, half : 2 * half],
        grad_o,
        small[0, :half],
        small[1, :half],
        small[2, :half],
        grad_up,
        small[0, 2 * half :],
        grad_down,
        small[3, :half],
        small[4, :half],
        small[5, :half],
    )


def solution(mesh):
    rows, cols, vec = P("head", None), P(None, "head"), P("head")
    tokens = P("dp", "blk", "head")
    return jax.shard_map(
        on_device,
        mesh=mesh,
        in_specs=(
            tokens, P("dp", None), rows, cols, vec, cols, cols, vec, rows, vec, vec, vec, cols,
            vec, rows, vec, vec, vec, tokens,
        ),
        out_specs=(
            tokens, tokens, cols, vec, cols, cols, vec, rows, vec, vec, vec, cols, vec, rows, vec,
            vec, vec,
        ),
        check_vma=False,
    )
```

profile of v0, /device:TPU:0, one launch (start us, length us, event | category | flops | bytes accessed | tf_op | source)
XLA Modules:
  0.0 252.8 jit_solution(18073208510348729760)
XLA Ops:
  0.7 0.7 reshape.59
  1.4 1.5 select_select_fusion.vec_own
  2.9 46.4 %front.1 = (bf16[1024,768]{1,0:T(8,128)(2,1)}, bf16[1024,768]{1,0:T(8,128)(2,1)}, bf16[1024,768]{1,0:T(8,128)(2,1)}, bf16[1024,768]{1,0:T(8,128)(2,1)}, bf16[102...) custom-call(bf16[2048,384]{1,0:T(8,128)(2,1)} %bitcast.6, ...), custom_call_target="tpu_custom_call" | custom-call | tf_op jit(solution)/shard_map/front/pallas_call | solution.py:262
  49.3 52.3 %middle.1 = (f32[1024,768]{1,0:T(8,128)}, f32[1024,768]{1,0:T(8,128)}, bf16[1024,768]{1,0:T(8,128)(2,1)}, bf16[1024,768]{1,0:T(8,128)(2,1)}, f32[8,768]{1,0:T(8,...) custom-call(bf16[1024,768]{1,0:T(8,128)(2,1)} %get-tuple-element.56.ctx_ref.ctx_hbm, ...), custom_call_target="tpu_custom_call" | custom-call | tf_op jit(solution)/shard_map/middle/pallas_call | solution.py:448
  101.6 135.3 %attention_back.1 = (bf16[768,1536]{1,0:T(8,128)(2,1)}, bf16[768,1536]{1,0:T(8,128)(2,1)}, bf16[768,1536]{1,0:T(8,128)(2,1)}, f32[8,2304]{1,0:T(8,128)}, f32[2048,384]{1,0:T(8,128)}, /*index=5*/f32[2048,384]{1,0:T(8,128)}) custom-call(bf16[768,1536]{1,0:T(8,128)(2,1)} %get-tuple-element.64.up_hbm, bf16[768,1536]{1,0:T(8,128)(2,1)} %get-tuple-element.65.down_hbm, ...), custom_call_target="tpu_custom_call" | custom-call | tf_op jit(solution)/shard_map/attention_back/pallas_call | solution.py:1105
  236.8 1.4 slice_reduce_fusion
  238.3 1.6 slice_reduce_fusion.1
  239.8 12.5 %finish.1 = (f32[768,1536]{1,0:T(8,128)}, f32[1536,768]{1,0:T(8,128)}, f32[768,384]{1,0:T(8,128)}, f32[768,384]{1,0:T(8,128)}, f32[768,384]{1,0:T(8,128)}, /*ind...) custom-call(bf16[768,1536]{1,0:T(8,128)(2,1)} %get-tuple-element.81.up_ref, ...), custom_call_target="tpu_custom_call" | custom-call | tf_op jit(solution)/shard_map/finish/pallas_call | solution.py:1153
  (4 shorter events, 0.0 us)
where the time goes:
time: 258 us; the launch traced here: 253 us
  Pallas kernels  246 us (95%)
  local copies, waits for them, and re-layouts  3.69 us (1%)
    pallas_call x1, Pallas kernels, attention_back(): pl.pallas_call(functools.partial(back_kernel, items, batches, groups, hea...  135 us
    pallas_call x1, Pallas kernels, middle(): pl.pallas_call(functools.partial(middle_kernel, chunk, tiles), grid=(tile...  52.3 us
    pallas_call x1, Pallas kernels, front(): pl.pallas_call(functools.partial(front_kernel, head_width, scale, seqs),...  46.4 us
    pallas_call x1, Pallas kernels, finish(): pl.pallas_call(functools.partial(finish_kernel, len(moved)), grid=(steps,...  12.5 us

commit v1 on v0

--- a/solution.py
+++ b/solution.py
@@ -231,14 +231,14 @@
         here = seq_rows(seq)
         for copy in cross[seq]:
             copy.wait_recv()
+        out.append(bring(18 + 4 * seq, xc_ref.at[here], xc_hbm.at[here]))
         x_cross = xc_ref[here, :]
         k_ref[here, half:] = dot(x_cross, ws_k[:, half:]).astype(BF16)
         v_ref[here, half:] = (dot(x_cross, ws_v[:, half:]) + bv[:, half:]).astype(BF16)
+        out.append(bring(19 + 4 * seq, k_ref.at[here], k_hbm.at[here]))
+        out.append(bring(20 + 4 * seq, v_ref.at[here], v_hbm.at[here]))
         attention(seq, pairs, 1)
-    out.append(bring(13, xc_ref, xc_hbm))
-    out.append(bring(14, k_ref, k_hbm))
-    out.append(bring(15, v_ref, v_hbm))
-    out.append(bring(16, ctx_ref, ctx_hbm))
+        out.append(bring(21 + 4 * seq, ctx_ref.at[here], ctx_hbm.at[here]))
     for copy in later:
         copy.wait_recv()
     for copy in out:
@@ -281,7 +281,7 @@
             pltpu.VMEM((8, half), F32),
             pltpu.VMEM((block_len, block_len), F32),
             pltpu.VMEM((rows, half), F32),
-            pltpu.SemaphoreType.DMA((18,)),
+            pltpu.SemaphoreType.DMA((18 + 4 * seqs,)),
             pltpu.SemaphoreType.DMA((copies,)),
             pltpu.SemaphoreType.DMA((copies,)),
         ],
@@ -484,11 +484,11 @@
 RATES = {"core": 500e3, "x": 46e3, "y": 46e3, "outer": 46e3, "inner": 46e3, "group": 46e3}
 DELAY = 4.5
 OP_TIME = 0.3
-URGENCY = 1.0
-AHEAD = 5.0
+URGENCY = 2.0
+AHEAD = 8.0
 ORDERS = {
     "A": "xyuw", "B": "yxuw", "C": "uwxy", "D": "uxyw", "E": "xuyw", "F": "yuxw", "G": "uyxw",
-    "H": "uwyx",
+    "H": "uwyx", "I": "xuwy", "J": "yuwx", "K": "uxwy", "L": "uywx",
 }
 
 
@@ -751,15 +751,11 @@
     return shapes
 
 
-def make_items(arrays, rows, cols, orders, groups, from_head, at=0):
-    items = []
-    step = len(arrays) * cols // len(orders)
-    for index in range(len(orders)):
-        array, first = divmod(index * step, cols)
-        items.append(
-            Item(at + index, arrays[array], first, step, rows, orders[index], groups, from_head)
-        )
-    return items
+def make_items(spans, rows, groups, from_head, at=0):
+    return [
+        Item(at + index, array, first, cols, rows, order, groups, from_head)
+        for index, (array, first, cols, order) in enumerate(spans)
+    ]
 
 
 def run_batch(sums, batch):
@@ -767,8 +763,8 @@
         sums.op(index, stage)
 
 
-FFN_ORDERS = "GGAAAFFB"
-HEAD_ORDERS = "DBDBBA"
+FFN_ORDERS = "LBBLBBAA"
+HEAD_ITEMS = [("o", 0, 3, "D"), ("v", 0, 3, "B"), ("k", 0, 3, "G"), ("q", 0, 3, "B")]
 MOVES = 4
 
 
@@ -1008,44 +1004,45 @@
     for at in (6, 7):
         loads[at].wait()
     steps(tokens // tile, cross_inputs)
-    steps(seqs * pairs // 2, functools.partial(attention, 0))
     for at in range(8, 13):
         loads[at].wait()
 
-    def weights(step):
-        mine = tile_of(step)
-        left, left_cross = x_ref[:, mine].T, xc_ref[:, mine].T
-        for at, ref in enumerate((q_ref, k_ref, v_ref)):
-            first = dot(left, ref[:, :half])
-            second = dot(left if at == 0 else left_cross, ref[:, half:])
-            found = jnp.concatenate([first, second], axis=1).astype(BF16)
-            natural = dot(found, sorter_ref[...], 1, 1).astype(BF16)
-            heads_own[mine, at * half : (at + 1) * half] = natural[:, :half]
-            heads_other[mine, at * half : (at + 1) * half] = natural[:, half:]
-        gwo_ref[mine, :] = dot(ctx_ref[:, mine].T, gattnb_ref[...]).astype(BF16)
-
-    steps(width // tile, weights)
-
-    def last_weight(_):
+    def out_weight(_):
+        @pl.loop(0, width // tile)
+        def _(at):
+            mine = tile_of(at)
+            gwo_ref[mine, :] = dot(ctx_ref[:, mine].T, gattnb_ref[...]).astype(BF16)
+
         for ref, low in ((heads_own, 0), (heads_other, half)):
             natural = dot(sorter_ref[low : low + half], gwo_ref[...]).astype(BF16)
             ref[:half, 3 * half :] = natural[:, :half]
             ref[half:, 3 * half :] = natural[:, half:]
+
+    steps(1, out_weight)
+    steps(seqs * pairs // 2, functools.partial(attention, 0))
+
+    def weight(kind, ref, left_cross, _):
+        @pl.loop(0, width // tile)
+        def _(at):
+            mine = tile_of(at)
+            first = dot(x_ref[:, mine].T, ref[:, :half])
+            second = dot(left_cross[:, mine].T, ref[:, half:])
+            found = jnp.concatenate([first, second], axis=1).astype(BF16)
+            natural = dot(found, sorter_ref[...], 1, 1).astype(BF16)
+            heads_own[mine, kind * half : (kind + 1) * half] = natural[:, :half]
+            heads_other[mine, kind * half : (kind + 1) * half] = natural[:, half:]
+
+    for kind, ref, left_cross in ((2, v_ref, xc_ref), (1, k_ref, xc_ref), (0, q_ref, x_ref)):
+        steps(1, functools.partial(weight, kind, ref, left_cross))
+
+    def vector_sums(_):
         totals = []
         for ref in (q_ref, v_ref):
             totals.append(jnp.sum(ref[...].astype(F32), axis=0, keepdims=True))
         found = jnp.concatenate(totals + [jnp.zeros((6, width), F32)], axis=0)
-        high = found.astype(BF16)
-        rest = found - high.astype(F32)
-        middle_part = rest.astype(BF16)
-        rest = rest - middle_part.astype(F32)
-        bsum_ref[...] = (
-            dot(high, sorter_ref[...], 1, 1)
-            + dot(middle_part, sorter_ref[...], 1, 1)
-            + dot(rest.astype(BF16), sorter_ref[...], 1, 1)
-        )
-
-    steps(1, last_weight)
+        bsum_ref[...] = split_dot(found, sorter_ref[...], 1, 1)
+
+    steps(1, vector_sums)
     rows_copy().start()
     for at in range(13, 15):
         loads[at].wait()
@@ -1074,29 +1071,37 @@
     rows, cols = grads[0].shape
     count, width = tokens[0].shape
     seqs = count // block_len
-    items = make_items([0, 1], rows, cols, FFN_ORDERS, groups, False)
-    items += make_items([2], rows, cols, HEAD_ORDERS, groups, True, len(items))
+    step = 2 * cols // len(FFN_ORDERS)
+    spans = [(*divmod(at * step, cols), step, order) for at, order in enumerate(FFN_ORDERS)]
+    items = make_items(spans, rows, groups, False)
+    quarter = cols // 4
+    spans = [
+        (2, "qkvo".index(kind) * quarter + low * quarter // 3, size * quarter // 3, order)
+        for kind, low, size, order in HEAD_ITEMS
+    ]
+    items += make_items(spans, rows, groups, True, len(items))
     pair_steps = seqs * width // (2 * head_width)
-    tiles, weight_steps = count // 256, width // 256
+    tiles = count // 256
     half_steps = pair_steps // 2
     times = (
-        [2.3] * half_steps + [0.9] * tiles + [2.3] * half_steps + [4.0] * weight_steps + [1.5]
+        [2.3] * half_steps + [0.9] * tiles + [3.0] + [2.3] * half_steps + [3.9] * 3 + [1.0]
         + [1.1] * tiles
     )
-    heads_at = pair_steps + tiles + weight_steps + 1
-    ready = [0] * len(FFN_ORDERS) + [heads_at] * len(HEAD_ORDERS)
+    after = pair_steps + tiles + 1
+    kind_ready = {"o": half_steps + tiles + 1, "v": after + 1, "k": after + 2, "q": after + 3}
+    ready = [0] * len(FFN_ORDERS) + [kind_ready[kind] for kind, _, _, _ in HEAD_ITEMS]
     small = (8, width + cols)
     items.append(Other([("head", 1e4)] + [(axis, 7e4) for axis in small_axes(groups)]))
-    ready.append(heads_at)
+    ready.append(after + 4)
     for at in range(MOVES):
         items.append(Other([("x", count // MOVES * width * 2), ("head", count // MOVES * width * 2)]))
-        items[-1].later = heads_at + (at + 1) * tiles // MOVES
+        items[-1].later = after + 4 + (at + 1) * tiles // MOVES
         ready.append(half_steps + (at + 1) * tiles // MOVES)
     batches = plan(items, times, ready)
     landing = landing_shapes(items)
     vmem = pl.BlockSpec(memory_space=pltpu.VMEM)
     anywhere = pl.BlockSpec(memory_space=pl.ANY)
-    slots = len(FFN_ORDERS) + len(HEAD_ORDERS)
+    slots = len(FFN_ORDERS) + len(HEAD_ITEMS)
     small_slots = 7 + groups - 1
     big = pltpu.VMEM((rows, cols), BF16)
     rows_low = pltpu.VMEM((count, width), BF16)

time: 258 us -> 256 us (level)
  no operation moved by 1% of the time
where the time goes in v1:
time: 256 us; the launch traced here: 251 us
  Pallas kernels  245 us (96%)
  local copies, waits for them, and re-layouts  3.69 us (1%)
    pallas_call x1, Pallas kernels, attention_back(): pl.pallas_call(functools.partial(back_kernel, items, batches, groups, hea...  134 us
    pallas_call x1, Pallas kernels, middle(): pl.pallas_call(functools.partial(middle_kernel, chunk, tiles), grid=(tile...  52.2 us
    pallas_call x1, Pallas kernels, front(): pl.pallas_call(functools.partial(front_kernel, head_width, scale, seqs),...  46.1 us
    pallas_call x1, Pallas kernels, finish(): pl.pallas_call(functools.partial(finish_kernel, len(moved)), grid=(steps,...  12.5 us

profile of v1, /device:TPU:0, one launch (start us, length us, event | category | flops | bytes accessed | tf_op | source)
XLA Modules:
  0.0 251.0 jit_solution(5959221839262678690)
XLA Ops:
  0.7 0.7 reshape.59
  1.4 1.5 select_select_fusion.vec_own
  2.9 46.1 %front.1 = (bf16[1024,768]{1,0:T(8,128)(2,1)}, bf16[1024,768]{1,0:T(8,128)(2,1)}, bf16[1024,768]{1,0:T(8,128)(2,1)}, bf16[1024,768]{1,0:T(8,128)(2,1)}, bf16[102...) custom-call(bf16[2048,384]{1,0:T(8,128)(2,1)} %bitcast.6, ...), custom_call_target="tpu_custom_call" | custom-call | tf_op jit(solution)/shard_map/front/pallas_call | solution.py:262
  49.0 52.2 %middle.1 = (f32[1024,768]{1,0:T(8,128)}, f32[1024,768]{1,0:T(8,128)}, bf16[1024,768]{1,0:T(8,128)(2,1)}, bf16[1024,768]{1,0:T(8,128)(2,1)}, f32[8,768]{1,0:T(8,...) custom-call(bf16[1024,768]{1,0:T(8,128)(2,1)} %get-tuple-element.56.ctx_ref.ctx_hbm, ...), custom_call_target="tpu_custom_call" | custom-call | tf_op jit(solution)/shard_map/middle/pallas_call | solution.py:448
  101.2 133.8 %attention_back.1 = (bf16[768,1536]{1,0:T(8,128)(2,1)}, bf16[768,1536]{1,0:T(8,128)(2,1)}, bf16[768,1536]{1,0:T(8,128)(2,1)}, f32[8,2304]{1,0:T(8,128)}, f32[2048,384]{1,0:T(8,128)}, /*index=5*/f32[2048,384]{1,0:T(8,128)}) custom-call(bf16[768,1536]{1,0:T(8,128)(2,1)} %get-tuple-element.64.up_hbm, bf16[768,1536]{1,0:T(8,128)(2,1)} %get-tuple-element.65.down_hbm, ...), custom_call_target="tpu_custom_call" | custom-call | tf_op jit(solution)/shard_map/attention_back/pallas_call | solution.py:1110
  235.0 1.4 slice_reduce_fusion
  236.4 1.6 slice_reduce_fusion.1
  238.0 12.5 %finish.1 = (f32[768,1536]{1,0:T(8,128)}, f32[1536,768]{1,0:T(8,128)}, f32[768,384]{1,0:T(8,128)}, f32[768,384]{1,0:T(8,128)}, f32[768,384]{1,0:T(8,128)}, /*ind...) custom-call(bf16[768,1536]{1,0:T(8,128)(2,1)} %get-tuple-element.81.up_ref, ...), custom_call_target="tpu_custom_call" | custom-call | tf_op jit(solution)/shard_map/finish/pallas_call | solution.py:1158
  (4 shorter events, 0.0 us)
